TPU v7x, 256 devices: a whole 4x4x8 slice. The times are simulated.
256 devices in a mesh: dp: 64 (over z, x, core), pipe: 4 (over y).
Axes of the slice: x: 4, y: 4, z: 8, core: 2. Of those that a mesh axis runs over, the one named last changes fastest.
Arguments:
- perturbed: bfloat16 [2, 4096, 4096], P(None, 'dp'), may hold values from -6 to 6
- control_token_states: bfloat16 [2, 4096, 4096], P(None, 'dp'), may hold values from -6 to 6
- owners: int32 [2, 4096, 1], P(None, 'dp'), may hold values from 0 to 63; in each aligned block of 64 rows (0 to 63, 64 to 127, ..., all dimensions but the last counted through in order) at most 4 rows name the same one
- matched_control_row: int32 [2, 4096], P(None, 'dp'), may hold values from 0 to 63
- cell_time_bins: int32 [2, 2], replicated, may hold values from 0 to 999
- frozen: bfloat16 [4, 4096, 2048], P('pipe', 'dp'), may hold values from -0.09375 to 0.09375
- section_norm_gain: float32 [4, 4096], P('pipe'), may hold values from 0.5 to 1.5
- adapter_into_rank: bfloat16 [4, 4096, 64], P('pipe'), may hold values from -0.09375 to 0.09375
- adapter_onto_hidden: bfloat16 [4, 64, 2048], P('pipe'), may hold values from -0.75 to 0.75
- adapter_hidden_to_rank: bfloat16 [4, 2048, 64], P('pipe'), may hold values from -0.125 to 0.125
- adapter_to_width: bfloat16 [4, 64, 4096], P('pipe'), may hold values from -0.75 to 0.75
Outputs:
- grad_gain: float32 [4, 4096], P('pipe')
- grad_in: float32 [4, 4096, 64], P('pipe')
- grad_up: float32 [4, 64, 2048], P('pipe')
- grad_mix: float32 [4, 2048, 64], P('pipe')
- grad_out: float32 [4, 64, 4096], P('pipe')
Inputs may be any that keep to these rules, and one draw needn't show every extreme that they name: `owners`: in each micro-batch, the 64 rows of one device of dp name no owner more than 4 times, a bound that some block reaches in some such rows.
All inputs are finite; a program needn't handle non-finite values.
Results may differ from a plain program's by a relative error of at most 0.0045.
Values may be sent and summed in bfloat16 or wider, within the bound.
No kernel may reach another device: no remote copies, remote signals or barrier semaphores. Data moves between devices by JAX's collectives and lax.ppermute only.
A program may use at most 128 MiB of HBM per device.

v0:
```python
import jax
import jax.numpy as jnp
from jax import lax
from jax.sharding import PartitionSpec as P

NBINS = 1000


epsilon = 1e-05


def passed_along(x, axis, by):
    size = lax.axis_size(axis)
    pairs = [(i, i + by) for i in range(size) if 0 <= i + by < size]
    return lax.ppermute(x, axis, pairs)


def times_transposed(left, right):
    return lax.dot_general(
        left, right, (((1,), (1,)), ((), ())), preferred_element_type=jnp.float32
    )


def transposed_times(left, right):
    return lax.dot_general(
        left, right, (((0,), (0,)), ((), ())), preferred_element_type=jnp.float32
    )


def time_features(t_val, width_dim):
    half_width = width_dim // 2
    frequency = jnp.exp(-jnp.log(10000.0) * jnp.arange(half_width, dtype=jnp.float32) / half_width)
    angles = (t_val * 1000.0)[:, None] * frequency[None, :]
    return jnp.concatenate([jnp.sin(angles), jnp.cos(angles)], axis=1)


def normalize(residual_state, gain_vector_row):
    hidden_widened = residual_state.astype(jnp.float32)
    inverse = lax.rsqrt(jnp.mean(hidden_widened * hidden_widened, axis=1, keepdims=True) + epsilon)
    normalized_state = (hidden_widened * inverse * gain_vector_row[None, :]).astype(jnp.bfloat16)
    return (hidden_widened, inverse, normalized_state)


def section_forward_pass(
    residual_state,
    gain_vector_row,
    frozen_weight_rows,
    adapter_down_first,
    adapter_up_first,
    adapter_down_second,
    adapter_up_second,
    frozen_matmul_result=None,
):
    hidden_widened, inverse, normalized_state = normalize(residual_state, gain_vector_row)
    rank_projected = jnp.dot(
        normalized_state, adapter_down_first, preferred_element_type=jnp.float32
    ).astype(jnp.bfloat16)
    frozen_matmul_result = jnp.dot(
        normalized_state, frozen_weight_rows, preferred_element_type=jnp.float32
    )
    mixed_preactivation = frozen_matmul_result + jnp.dot(
        rank_projected, adapter_up_first, preferred_element_type=jnp.float32
    )
    hidden_units_value = jax.nn.silu(mixed_preactivation).astype(jnp.bfloat16)
    rank_squeezed = jnp.dot(
        hidden_units_value, adapter_down_second, preferred_element_type=jnp.float32
    ).astype(jnp.bfloat16)
    section_result = (
        hidden_widened
        + jnp.dot(rank_squeezed, adapter_up_second, preferred_element_type=jnp.float32)
    ).astype(jnp.bfloat16)
    return (
        section_result,
        (
            inverse,
            normalized_state,
            rank_projected,
            mixed_preactivation,
            hidden_units_value,
            rank_squeezed,
        ),
    )


def section_backward_pass(
    residual_state,
    saved_activations,
    upstream_gradient,
    gain_vector_row,
    frozen_weight_rows,
    adapter_down_first,
    adapter_up_first,
    adapter_down_second,
    adapter_up_second,
):
    (
        inverse,
        normalized_state,
        rank_projected,
        mixed_preactivation,
        hidden_units_value,
        rank_squeezed,
    ) = saved_activations
    grad_e = transposed_times(rank_squeezed, upstream_gradient)
    squeezed_gradient = times_transposed(upstream_gradient, adapter_up_second).astype(jnp.bfloat16)
    grad_c = transposed_times(hidden_units_value, squeezed_gradient)
    hidden_gradient = times_transposed(squeezed_gradient, adapter_down_second)
    sigmoid_val = jax.nn.sigmoid(mixed_preactivation)
    preact_gradient = (
        hidden_gradient * sigmoid_val * (1.0 + mixed_preactivation * (1.0 - sigmoid_val))
    ).astype(jnp.bfloat16)
    grad_b = transposed_times(rank_projected, preact_gradient)
    lowered_gradient = times_transposed(preact_gradient, adapter_up_first).astype(jnp.bfloat16)
    grad_a = transposed_times(normalized_state, lowered_gradient)
    normed_gradient = times_transposed(preact_gradient, frozen_weight_rows) + times_transposed(
        lowered_gradient, adapter_down_first
    )
    unit_rows = residual_state.astype(jnp.float32) * inverse
    grad_g = jnp.sum(normed_gradient * unit_rows, axis=0)
    d_unit = normed_gradient * gain_vector_row[None, :]
    d_stream = inverse * (d_unit - unit_rows * jnp.mean(d_unit * unit_rows, axis=1, keepdims=True))
    upstream = (upstream_gradient.astype(jnp.float32) + d_stream).astype(jnp.bfloat16)
    return (upstream, (grad_g, grad_a, grad_b, grad_c, grad_e))


def send_forward(section_result):
    return passed_along(section_result, "pipe", 1)


def send_backward(upstream):
    return passed_along(upstream, "pipe", -1)


def per_device(
    perturbed,
    control_token_states,
    owners,
    matched_control_row,
    cell_time_bins,
    frozen,
    section_norm_gain,
    adapter_into_rank,
    adapter_onto_hidden,
    adapter_hidden_to_rank,
    adapter_to_width,
):
    micro_count = perturbed.shape[0]
    row_count = perturbed.shape[1]
    width_dim = perturbed.shape[2]
    peer_count = lax.axis_size("dp")
    sections = lax.axis_size("pipe")
    relay_section_index = lax.axis_index("pipe")
    capacity = 4 * row_count // peer_count
    pool_flat = control_token_states.reshape(micro_count * row_count, width_dim)
    cell_count = cell_time_bins.shape[1]
    cell_length = row_count * peer_count // cell_count

    def build_requests(batch_index):
        owner_ids = owners[batch_index, :, 0]
        onehot = (owner_ids[:, None] == jnp.arange(peer_count, dtype=jnp.int32)[None, :]).astype(
            jnp.int32
        )
        slot_rank = jnp.sum((jnp.cumsum(onehot, axis=0) - onehot) * onehot, axis=1)
        row_ids = batch_index * row_count + matched_control_row[batch_index]
        request_table = (
            jnp.zeros((peer_count, capacity), jnp.int32).at[owner_ids, slot_rank].set(row_ids)
        )
        return (owner_ids, slot_rank, request_table)

    first_product = None
    complete_rows = lax.all_gather(frozen[0], "dp", axis=0, tiled=True)
    request_plans = [build_requests(batch_index) for batch_index in range(micro_count)]
    gathered_rows = []
    for batch_index in range(micro_count):
        owner_ids, slot_rank, request_table = request_plans[batch_index]
        fetched = jnp.take(
            pool_flat,
            lax.all_to_all(request_table, "dp", split_axis=0, concat_axis=0, tiled=True),
            axis=0,
        )
        arrived = lax.all_to_all(fetched, "dp", split_axis=0, concat_axis=0, tiled=True)
        gathered_rows.append(arrived[owner_ids, slot_rank])
    position = lax.axis_index("dp") * row_count + jnp.arange(row_count, dtype=jnp.int32)
    member = (
        (position // cell_length)[:, None] == jnp.arange(cell_count, dtype=jnp.int32)[None, :]
    ).astype(jnp.int32)
    made_inputs = []
    made_velocities = []
    for batch_index in range(micro_count):
        bin_vals = jnp.sum(member * cell_time_bins[batch_index][None, :], axis=1)
        t_val = (bin_vals.astype(jnp.float32) + 0.5) / NBINS
        source_rows = gathered_rows[batch_index].astype(jnp.float32)
        target_rows = perturbed[batch_index].astype(jnp.float32)
        made_inputs.append(
            (
                (1.0 - t_val)[:, None] * source_rows
                + t_val[:, None] * target_rows
                + time_features(t_val, width_dim)
            ).astype(jnp.bfloat16)
        )
        made_velocities.append(target_rows - source_rows)
    relay_section_weights = (
        section_norm_gain[0],
        complete_rows,
        adapter_into_rank[0],
        adapter_onto_hidden[0],
        adapter_hidden_to_rank[0],
        adapter_to_width[0],
    )
    loss_scale = (micro_count * row_count * peer_count) ** (-0.5)
    tick_count = micro_count + sections - 1
    received = jnp.zeros((row_count, width_dim), jnp.bfloat16)
    stacked = []
    outputs = []
    for tick_index in range(tick_count):
        entry_rows = made_inputs[min(tick_index, micro_count - 1)]
        current = jnp.where(relay_section_index == 0, entry_rows, received)
        if tick_index == 0:
            section_result, saved_activations = section_forward_pass(
                current, *relay_section_weights, frozen_matmul_result=first_product
            )
        else:
            section_result, saved_activations = section_forward_pass(
                current, *relay_section_weights
            )
        stacked.append((current, saved_activations))
        outputs.append(section_result)
        if tick_index + 1 < tick_count:
            received = send_forward(section_result)
    history = jax.tree.map(lambda *leaves: jnp.stack(leaves), *stacked)
    out_stack = jnp.stack(outputs)
    gradient_totals = (
        jnp.zeros(section_norm_gain.shape[1:], jnp.float32),
        jnp.zeros(adapter_into_rank.shape[1:], jnp.float32),
        jnp.zeros(adapter_onto_hidden.shape[1:], jnp.float32),
        jnp.zeros(adapter_hidden_to_rank.shape[1:], jnp.float32),
        jnp.zeros(adapter_to_width.shape[1:], jnp.float32),
    )
    received = jnp.zeros((row_count, width_dim), jnp.bfloat16)
    for tick_index in range(tick_count):
        batch_slot = tick_index - (sections - 1 - relay_section_index)
        active = (batch_slot >= 0) & (batch_slot < micro_count)
        forward_tick = jnp.clip(
            tick_index - sections + 1 + 2 * relay_section_index, 0, tick_count - 1
        )
        current, saved_activations = jax.tree.map(lambda leaves: leaves[forward_tick], history)
        if tick_index < micro_count:
            prediction = out_stack[forward_tick]
            loss_seed = (
                (prediction.astype(jnp.float32) - made_velocities[tick_index]) * loss_scale
            ).astype(jnp.bfloat16)
            upstream_gradient = jnp.where(relay_section_index == sections - 1, loss_seed, received)
        else:
            upstream_gradient = received
        upstream, grad_terms = section_backward_pass(
            current, saved_activations, upstream_gradient, *relay_section_weights
        )
        gradient_totals = tuple(
            (
                jnp.where(active, gradient_totals[k] + grad_terms[k], gradient_totals[k])
                for k in range(5)
            )
        )
        if tick_index + 1 < tick_count:
            received = send_backward(upstream)
    summed = lax.psum(
        (
            gradient_totals[0],
            gradient_totals[1],
            gradient_totals[2],
            gradient_totals[3],
            gradient_totals[4],
        ),
        "dp",
    )
    return tuple((summed_item[None] for summed_item in summed))


def solution(mesh):
    in_specs = (
        P(None, "dp", None),
        P(None, "dp", None),
        P(None, "dp", None),
        P(None, "dp"),
        P(),
        P("pipe", "dp", None),
        P("pipe", None),
        P("pipe", None, None),
        P("pipe", None, None),
        P("pipe", None, None),
        P("pipe", None, None),
    )
    out_specs = (
        P("pipe", None),
        P("pipe", None, None),
        P("pipe", None, None),
        P("pipe", None, None),
        P("pipe", None, None),
    )
    return jax.shard_map(
        per_device, mesh=mesh, in_specs=in_specs, out_specs=out_specs, check_vma=False
    )
```

profile of v0, /device:TPU:1, one launch (start us, length us, event | category | flops | bytes accessed | tf_op | source)
XLA Modules:
  0.0 664.2 jit_solution(18247854657470036206)
XLA Ops:
  10.6 3.5 scatter_fusion
  14.8 13.0 %all-to-all-start = ((s32[64,1,4]{2,1,0:T(1,128)}), s32[64,1,4]{2,1,0:T(1,128)S(1)}, u32[]{:S(2)}, u32[]{:S(2)}) async-start(s32[64,1,4]{2,1,0:T(1,128)} %copy.24), calls=%async_computation | async-start | bytes 65536 | tf_op jit(solution)/shard_map/all_to_all | solution.py:178
  27.8 3.5 scatter_fusion.1
  32.0 5.2 all-to-all-done
  37.2 5.1 all-to-all-start.2
  46.6 4.0 broadcast_select_fusion.1
  51.6 9.7 %all-to-all-start.1 = ((bf16[64,4,4096]{2,1,0:T(4,128)(2,1)}), bf16[64,4,4096]{2,1,0:T(4,128)(2,1)S(1)}, u32[]{:S(2)}, u32[]{:S(2)}) async-start(bf16[64,4,4096]{2,1,0:T(4,128)(2,1)} %broadcast_select_fusion.1), calls=%async_computation.1 | async-start | bytes 4194304 | tf_op jit(solution)/shard_map/all_to_all | solution.py:181
  64.4 4.8 multiply_sine_fusion
  72.5 4.1 reshape.552
  76.6 4.0 broadcast_select_fusion
  80.6 49.6 %all-to-all-done.1 = bf16[64,4,4096]{2,1,0:T(4,128)(2,1)S(1)} async-done(((bf16[64,4,4096]{2,1,0:T(4,128)(2,1)}), bf16[64,4,4096]{2,1,0:T(4,128)(2,1)S(1)}, u32[]{:S(2)}, u32[]{:S(2)}) %all-to-all-start.1) | async-done | bytes 2097184 | tf_op jit(solution)/shard_map/all_to_all | solution.py:181
  130.2 8.8 %all-to-all-start.3 = ((bf16[64,4,4096]{2,1,0:T(4,128)(2,1)}), bf16[64,4,4096]{2,1,0:T(4,128)(2,1)}, u32[]{:S(2)}, u32[]{:S(2)}) async-start(bf16[64,4,4096]{2,1,0:T(4,128)(2,1)} %broadcast_select_fusion), calls=%async_computation.3 | async-start | bytes 4194304 | tf_op jit(solution)/shard_map/all_to_all | solution.py:181
  146.0 20.5 %all-gather.3.cloned.1.call-done = bf16[1,4096,2048]{2,1,0:T(8,128)(2,1)} async-done(((bf16[1,64,2048]{2,1,0:T(8,128)(2,1)}), bf16[1,4096,2048]{2,1,0:T(8,128)(2,1)}) %all-gather.3.cloned.1.call-update) | async-done | bytes 16777232 | tf_op jit(solution)/shard_map/all_gather | solution.py:171
  166.5 8.9 %fusion.18 = f32[64,2048]{1,0:T(8,128)S(1)} fusion(bf16[1,4096,2048]{2,1,0:T(8,128)(2,1)} %all-gather.3.cloned.1.call-done, bf16[64,4096]{1,0:T(8,128)(2,1)S(1)} %get-tuple-element.34, f32[4096]{0:T(1024)S(1)} %bitcast.592, f32[64]{0:T(128)S(1)} %add_rsqrt_fusion.4), kind=kOutput, calls=%fused_computation.24 | convolution fusion | flops 1074790400 | bytes 17842432 | tf_op jit(solution)/shard_map/dot_general | solution.py:58
  178.8 4.4 collective-permute-start
  183.2 13.0 %all-to-all-done.3 = bf16[64,4,4096]{2,1,0:T(4,128)(2,1)} async-done(((bf16[64,4,4096]{2,1,0:T(4,128)(2,1)}), bf16[64,4,4096]{2,1,0:T(4,128)(2,1)}, u32[]{:S(2)}, u32[]{:S(2)}) %all-to-all-start.3) | async-done | bytes 2097184 | tf_op jit(solution)/shard_map/all_to_all | solution.py:181
  196.2 3.4 gather_fusion.1
  203.3 9.0 %fusion.16 = f32[64,2048]{1,0:T(8,128)S(1)} fusion(bf16[1,4096,2048]{2,1,0:T(8,128)(2,1)} %all-gather.3.cloned.1.call-done, bf16[64,4096]{1,0:T(8,128)(2,1)S(1)} %get-tuple-element.29, f32[64]{0:T(128)S(1)} %add_rsqrt_fusion.3, f32[4096]{0:T(1024)S(1)} %bitcast.595), kind=kOutput, calls=%fused_computation.22 | convolution fusion | flops 1074790400 | bytes 17842432 | tf_op jit(solution)/shard_map/dot_general | solution.py:58
  218.1 9.7 %collective-permute-done.1 = bf16[64,4096]{1,0:T(8,128)(2,1)S(1)} collective-permute-done((bf16[64,4096]{1,0:T(8,128)(2,1)S(1)}, bf16[64,4096]{1,0:T(8,128)(2,1)S(1)}, u32[]{:S(2)}, u32[]{:S(2)}) %collective-permute-start.1) | collective-permute-done | bytes 524320 | tf_op jit(solution)/shard_map/ppermute | solution.py:15
  233.5 4.1 collective-permute-start.2
  237.8 8.8 %collective-permute-done.2 = bf16[64,4096]{1,0:T(8,128)(2,1)S(1)} collective-permute-done((bf16[64,4096]{1,0:T(8,128)(2,1)S(1)}, bf16[64,4096]{1,0:T(8,128)(2,1)S(1)}, u32[]{:S(2)}, u32[]{:S(2)}) %collective-permute-start.2) | collective-permute-done | bytes 524320 | tf_op jit(solution)/shard_map/ppermute | solution.py:15
  252.3 4.3 collective-permute-start.3
  256.7 7.7 %collective-permute-done.3 = bf16[64,4096]{1,0:T(8,128)(2,1)S(1)} collective-permute-done((bf16[64,4096]{1,0:T(8,128)(2,1)S(1)}, bf16[64,4096]{1,0:T(8,128)(2,1)S(1)}, u32[]{:S(2)}, u32[]{:S(2)}) %collective-permute-start.3) | collective-permute-done | bytes 524320 | tf_op jit(solution)/shard_map/ppermute | solution.py:15
  272.8 11.9 %fusion.8 = f32[64,4096]{1,0:T(8,128)} fusion(bf16[64,2048]{1,0:T(8,128)(2,1)S(1)} %fusion.57, bf16[1,4096,2048]{2,1,0:T(8,128)(2,1)} %all-gather.3.cloned.1.call-done), kind=kOutput, calls=%fused_computation.14 | convolution fusion | flops 1073741824 | bytes 18087936 | tf_op jit(solution)/shard_map/dot_general | solution.py:19
  295.1 5.8 collective-permute-done.4
  304.1 10.9 %fusion.6 = f32[64,4096]{1,0:T(8,128)S(1)} fusion(bf16[64,2048]{1,0:T(8,128)(2,1)S(1)} %fusion.56, bf16[1,4096,2048]{2,1,0:T(8,128)(2,1)} %all-gather.3.cloned.1.call-done), kind=kOutput, calls=%fused_computation.12 | convolution fusion | flops 1073741824 | bytes 18087936 | tf_op jit(solution)/shard_map/dot_general | solution.py:19
  325.3 3.5 collective-permute-done.5
  330.7 10.9 %fusion.4 = f32[64,4096]{1,0:T(8,128)S(1)} fusion(bf16[64,2048]{1,0:T(8,128)(2,1)S(1)} %fusion.55, bf16[1,4096,2048]{2,1,0:T(8,128)(2,1)} %all-gather.3.cloned.1.call-done), kind=kOutput, calls=%fused_computation.10 | convolution fusion | flops 1073741824 | bytes 18087936 | tf_op jit(solution)/shard_map/dot_general | solution.py:19
  356.7 10.9 %fusion.2 = f32[64,4096]{1,0:T(8,128)S(1)} fusion(bf16[64,2048]{1,0:T(8,128)(2,1)S(1)} %fusion.54, bf16[1,4096,2048]{2,1,0:T(8,128)(2,1)} %all-gather.3.cloned.1.call-done), kind=kOutput, calls=%fused_computation.8 | convolution fusion | flops 1073741824 | bytes 18087936 | tf_op jit(solution)/shard_map/dot_general | solution.py:19
  375.6 5.3 collective-permute-done.7
  389.5 10.9 %fusion = f32[64,4096]{1,0:T(8,128)S(1)} fusion(bf16[64,2048]{1,0:T(8,128)(2,1)S(1)} %fusion.53, bf16[1,4096,2048]{2,1,0:T(8,128)(2,1)} %all-gather.3.cloned.1.call-done), kind=kOutput, calls=%fused_computation.6 | convolution fusion | flops 1073741824 | bytes 18087936 | tf_op jit(solution)/shard_map/dot_general | solution.py:19
  401.9 248.9 %psum.35 = f32[1,4096]{1,0:T(1,128)} all-reduce(f32[1,4096]{1,0:T(1,128)S(1)} %bitcast.619), channel_id=1, replica_groups=mesh['dp'=64,'pipe'=4] {'dp'}, use_global_device_ids=true, to_apply=%region_22.24 | all-reduce | flops 4096 | bytes 32768 | tf_op jit(solution)/shard_map/psum | solution.py:266
  (238 shorter events, 120.0 us)
Async XLA Ops:
  7.2 35.3 %copy-start = (bf16[2,64,4096]{2,1,0:T(8,128)(2,1)S(1)}, bf16[2,64,4096]{2,1,0:T(8,128)(2,1)}, u32[]{:S(2)}) copy-start(bf16[2,64,4096]{2,1,0:T(8,128)(2,1)} %param.14) | copy-start | bytes 3145732
  7.2 159.3 %all-gather.3.cloned.1.call-start = ((), (), s32[]{:S(2)}) async-start(), calls=%async_computation.4 | async-start | bytes 17039360 | tf_op jit(solution)/shard_map/all_gather | solution.py:171
  14.8 22.4 %all-to-all-start = ((s32[64,1,4]{2,1,0:T(1,128)}), s32[64,1,4]{2,1,0:T(1,128)S(1)}, u32[]{:S(2)}, u32[]{:S(2)}) async-start(s32[64,1,4]{2,1,0:T(1,128)} %copy.24), calls=%async_computation | async-start | bytes 65536 | tf_op jit(solution)/shard_map/all_to_all | solution.py:178
  37.2 14.4 %all-to-all-start.2 = ((s32[64,1,4]{2,1,0:T(1,128)}), s32[64,1,4]{2,1,0:T(1,128)S(1)}, u32[]{:S(2)}, u32[]{:S(2)}) async-start(s32[64,1,4]{2,1,0:T(1,128)} %copy.25), calls=%async_computation.2 | async-start | bytes 65536 | tf_op jit(solution)/shard_map/all_to_all | solution.py:178
  50.6 10.8 %copy-start.31 = (s32[2,2]{1,0:T(2,128)S(1)}, s32[2,2]{1,0:T(2,128)}, u32[]{:S(2)}) copy-start(s32[2,2]{1,0:T(2,128)} %param.17) | copy-start | bytes 52
  51.6 78.6 %all-to-all-start.1 = ((bf16[64,4,4096]{2,1,0:T(4,128)(2,1)}), bf16[64,4,4096]{2,1,0:T(4,128)(2,1)S(1)}, u32[]{:S(2)}, u32[]{:S(2)}) async-start(bf16[64,4,4096]{2,1,0:T(4,128)(2,1)} %broadcast_select_fusion.1), calls=%async_computation.1 | async-start | bytes 4194304 | tf_op jit(solution)/shard_map/all_to_all | solution.py:181
  130.2 66.0 %all-to-all-start.3 = ((bf16[64,4,4096]{2,1,0:T(4,128)(2,1)}), bf16[64,4,4096]{2,1,0:T(4,128)(2,1)}, u32[]{:S(2)}, u32[]{:S(2)}) async-start(bf16[64,4,4096]{2,1,0:T(4,128)(2,1)} %broadcast_select_fusion), calls=%async_computation.3 | async-start | bytes 4194304 | tf_op jit(solution)/shard_map/all_to_all | solution.py:181
  139.0 511.8 %all-reduce.3.cloned.1.call-start = ((), (), s32[]{:S(2)}) async-start(), calls=%async_computation.5 | async-start | bytes 6291456 | tf_op jit(solution)/shard_map/psum | solution.py:266
  166.5 8.9 %copy-start.3 = (bf16[1,64,2048]{2,1,0:T(8,128)(2,1)S(1)}, bf16[1,64,2048]{2,1,0:T(8,128)(2,1)}, u32[]{:S(2)}) copy-start(bf16[1,64,2048]{2,1,0:T(8,128)(2,1)} %param.21) | copy-start | bytes 786436
  166.5 10.8 %copy-start.32 = (bf16[1,2048,64]{1,2,0:T(8,128)(2,1)S(1)}, bf16[1,2048,64]{1,2,0:T(8,128)(2,1)}, u32[]{:S(2)}) copy-start(bf16[1,2048,64]{1,2,0:T(8,128)(2,1)} %param.22) | copy-start | bytes 786436
  178.8 20.8 %copy-start.17 = (f32[64,2048]{1,0:T(8,128)S(1)}, f32[64,2048]{1,0:T(8,128)}, u32[]{:S(2)}) copy-start(f32[64,2048]{1,0:T(8,128)} %copy-done.16) | copy-start | bytes 1572868
  178.8 21.0 %collective-permute-start = (bf16[64,4096]{1,0:T(8,128)(2,1)}, bf16[64,4096]{1,0:T(8,128)(2,1)}, u32[]{:S(2)}, u32[]{:S(2)}) collective-permute-start(bf16[64,4096]{1,0:T(8,128)(2,1)} %get-tuple-element.65), channel_id=1, source_target_pairs={{0,1},{1,2},{2,3},{4,5},{5,6},{6,7},{8,9},{9,10},{10,11},{12,13},{... | collective-permute-start | bytes 1572872 | tf_op jit(solution)/shard_map/ppermute | solution.py:15
  203.3 9.1 %copy-start.29 = (f32[5,64,2048]{2,1,0:T(8,128)S(1)}, f32[5,64,2048]{2,1,0:T(8,128)}, u32[]{:S(2)}) copy-start(f32[5,64,2048]{2,1,0:T(8,128)} %get-tuple-element.72) | copy-start | bytes 7864324
  203.3 9.3 %copy-start.33 = (bf16[1,2048,64]{1,2,0:T(8,128)(2,1)S(1)}, bf16[1,2048,64]{1,2,0:T(8,128)(2,1)}, u32[]{:S(2)}) copy-start(bf16[1,2048,64]{1,2,0:T(8,128)(2,1)} %param.22) | copy-start | bytes 786436
  203.3 26.2 %slice-start = ((s8[16777216]{0:T(1024)(128)(4,1)}), s8[4194304]{0:T(1024)(128)(4,1)S(1)}, s32[]{:S(2)}) async-start(s8[16777216]{0:T(1024)(128)(4,1)} %bitcast.586), calls=%async_computation.6 | async-start | bytes 8388608
  203.3 26.2 %slice-start.1 = ((s8[16777216]{0:T(1024)(128)(4,1)}), s8[4194304]{0:T(1024)(128)(4,1)S(1)}, s32[]{:S(2)}) async-start(s8[16777216]{0:T(1024)(128)(4,1)} %bitcast.586), calls=%async_computation.7 | async-start | bytes 8388608
  203.3 26.2 %slice-start.2 = ((s8[16777216]{0:T(1024)(128)(4,1)}), s8[4194304]{0:T(1024)(128)(4,1)S(1)}, s32[]{:S(2)}) async-start(s8[16777216]{0:T(1024)(128)(4,1)} %bitcast.586), calls=%async_computation.8 | async-start | bytes 8388608
  212.6 16.9 %slice-start.3 = ((s8[16777216]{0:T(1024)(128)(4,1)}), s8[4194304]{0:T(1024)(128)(4,1)S(1)}, s32[]{:S(2)}) async-start(s8[16777216]{0:T(1024)(128)(4,1)} %bitcast.586), calls=%async_computation.9 | async-start | bytes 8388608
  214.5 13.3 %collective-permute-start.1 = (bf16[64,4096]{1,0:T(8,128)(2,1)S(1)}, bf16[64,4096]{1,0:T(8,128)(2,1)S(1)}, u32[]{:S(2)}, u32[]{:S(2)}) collective-permute-start(bf16[64,4096]{1,0:T(8,128)(2,1)S(1)} %get-tuple-element.67), channel_id=1, source_target_pairs={{0,1},{1,2},{2,3},{4,5},{5,6},{6,7},{8,9},{9,10},{10,11},{12,13},{... | collective-permute-start | bytes 1572872 | tf_op jit(solution)/shard_map/ppermute | solution.py:15
  233.5 13.1 %collective-permute-start.2 = (bf16[64,4096]{1,0:T(8,128)(2,1)S(1)}, bf16[64,4096]{1,0:T(8,128)(2,1)S(1)}, u32[]{:S(2)}, u32[]{:S(2)}) collective-permute-start(bf16[64,4096]{1,0:T(8,128)(2,1)S(1)} %get-tuple-element.69), channel_id=1, source_target_pairs={{0,1},{1,2},{2,3},{4,5},{5,6},{6,7},{8,9},{9,10},{10,11},{12,13},{... | collective-permute-start | bytes 1572872 | tf_op jit(solution)/shard_map/ppermute | solution.py:15
  252.3 12.2 %collective-permute-start.3 = (bf16[64,4096]{1,0:T(8,128)(2,1)S(1)}, bf16[64,4096]{1,0:T(8,128)(2,1)S(1)}, u32[]{:S(2)}, u32[]{:S(2)}) collective-permute-start(bf16[64,4096]{1,0:T(8,128)(2,1)S(1)} %get-tuple-element.71), channel_id=1, source_target_pairs={{0,1},{1,2},{2,3},{4,5},{5,6},{6,7},{8,9},{9,10},{10,11},{12,13},{... | collective-permute-start | bytes 1572872 | tf_op jit(solution)/shard_map/ppermute | solution.py:15
  288.4 12.5 %copy-start.9 = (bf16[64,4096]{1,0:T(8,128)(2,1)S(1)}, bf16[64,4096]{1,0:T(8,128)(2,1)}, u32[]{:S(2)}) copy-start(bf16[64,4096]{1,0:T(8,128)(2,1)} %gather_fusion.1) | copy-start | bytes 1572868
  288.4 12.5 %collective-permute-start.4 = (bf16[64,4096]{1,0:T(8,128)(2,1)S(1)}, bf16[64,4096]{1,0:T(8,128)(2,1)S(1)}, u32[]{:S(2)}, u32[]{:S(2)}) collective-permute-start(bf16[64,4096]{1,0:T(8,128)(2,1)S(1)} %fusion.128), channel_id=1, source_target_pairs={{1,0},{2,1},{3,2},{5,4},{6,5},{7,6},{9,8},{10,9},{11,10},{13,12},{... | collective-permute-start | bytes 1572872 | tf_op jit(solution)/shard_map/ppermute | solution.py:15
  293.7 8.8 %copy-start.34 = (bf16[1,2048,64]{1,2,0:T(8,128)(2,1)S(1)}, bf16[1,2048,64]{1,2,0:T(8,128)(2,1)}, u32[]{:S(2)}) copy-start(bf16[1,2048,64]{1,2,0:T(8,128)(2,1)} %param.22) | copy-start | bytes 786436
  318.1 6.9 %copy-start.13 = (f32[64,4096]{1,0:T(8,128)S(1)}, f32[64,4096]{1,0:T(8,128)}, u32[]{:S(2)}) copy-start(f32[64,4096]{1,0:T(8,128)} %convolution_select_fusion) | copy-start | bytes 3145732
  318.1 10.8 %collective-permute-start.5 = (bf16[64,4096]{1,0:T(8,128)(2,1)S(1)}, bf16[64,4096]{1,0:T(8,128)(2,1)S(1)}, u32[]{:S(2)}, u32[]{:S(2)}) collective-permute-start(bf16[64,4096]{1,0:T(8,128)(2,1)S(1)} %fusion.119), channel_id=1, source_target_pairs={{1,0},{2,1},{3,2},{5,4},{6,5},{7,6},{9,8},{10,9},{11,10},{13,12},{... | collective-permute-start | bytes 1572872 | tf_op jit(solution)/shard_map/ppermute | solution.py:15
  322.9 6.2 copy-start.35
  344.8 10.1 %collective-permute-start.6 = (bf16[64,4096]{1,0:T(8,128)(2,1)S(1)}, bf16[64,4096]{1,0:T(8,128)(2,1)S(1)}, u32[]{:S(2)}, u32[]{:S(2)}) collective-permute-start(bf16[64,4096]{1,0:T(8,128)(2,1)S(1)} %fusion.110), channel_id=1, source_target_pairs={{1,0},{2,1},{3,2},{5,4},{6,5},{7,6},{9,8},{10,9},{11,10},{13,12},{... | collective-permute-start | bytes 1572872 | tf_op jit(solution)/shard_map/ppermute | solution.py:15
  349.9 5.2 copy-start.36
  370.9 10.1 %collective-permute-start.7 = (bf16[64,4096]{1,0:T(8,128)(2,1)S(1)}, bf16[64,4096]{1,0:T(8,128)(2,1)S(1)}, u32[]{:S(2)}, u32[]{:S(2)}) collective-permute-start(bf16[64,4096]{1,0:T(8,128)(2,1)S(1)} %fusion.101), channel_id=1, source_target_pairs={{1,0},{2,1},{3,2},{5,4},{6,5},{7,6},{9,8},{10,9},{11,10},{13,12},{... | collective-permute-start | bytes 1572872 | tf_op jit(solution)/shard_map/ppermute | solution.py:15
  374.0 7.2 %copy-start.37 = (bf16[1,2048,64]{1,2,0:T(8,128)(2,1)S(1)}, bf16[1,2048,64]{1,2,0:T(8,128)(2,1)}, u32[]{:S(2)}) copy-start(bf16[1,2048,64]{1,2,0:T(8,128)(2,1)} %param.22) | copy-start | bytes 786436
  650.9 6.1 copy-start.1
  (24 other events, 76.2 us)
Sparse Core Ops, SparseCore 0:
  10.8 155.6 all-gather.2
  389.7 203.7 all-reduce.2
where the time goes:
time: 676 us; the launch traced here: 664 us
  blocking collectives  249 us (37%)
  waiting for transfers between devices  133 us (20%)
  matrix products  133 us (20%)
  starting transfers between devices  59 us (9%)
  local copies, waits for them, and re-layouts  37 us (5%)
  other arithmetic  36.7 us (5%)
  between operations  15.7 us (2%)
    psum x1, blocking collectives, per_device(): lax.psum((gradient_totals[0], gradient_totals[1], gradient_totals[2], gra...  249 us
    dot_general x25, matrix products, times_transposed(): lax.dot_general(left, right, (((1,), (1,)), ((), ())), preferred_element_...  72 us
    all_to_all x2, waiting for transfers between devices, per_device(): lax.all_to_all(fetched, 'dp', split_axis=0, concat_axis=0, tiled=True)  62.6 us
    ppermute x8, waiting for transfers between devices, passed_along(): return lax.ppermute(x, axis, pairs)  43.3 us
    dot_general x5, matrix products, section_forward_pass(): jnp.dot(normalized_state, frozen_weight_rows, preferred_element_type=jnp....  27.3 us
    dot_general x20, matrix products, transposed_times(): lax.dot_general(left, right, (((0,), (0,)), ((), ())), preferred_element_...  26.8 us
    ppermute x8, starting transfers between devices, passed_along(): return lax.ppermute(x, axis, pairs)  22.4 us
    all_gather x1, waiting for transfers between devices, per_device(): complete_rows = lax.all_gather(frozen[0], 'dp', axis=0, tiled=True)  20.5 us
  transfers between devices with their start and end apart: 14, of which 12 were waited for; matrix products, arithmetic and copies ran while one was open for 14% of the time, Pallas kernels for 0%

commit v1 on v0

v1 whole, which is shorter than its diff:
```python
import jax
import jax.numpy as jnp
from jax import lax
from jax.experimental import pallas as pl
from jax.experimental.pallas import tpu as pltpu
from jax.sharding import Mesh
from jax.sharding import PartitionSpec as P

NBINS = 1000
EPSILON = 1e-05
TOKENS = 128
WIDTH = 4096
HIDDEN = 2048
RANK = 64
SECTIONS = 4
WIDE = 512
NARROW = 256
DP = ("z", "x", "core")
F32 = jnp.float32
BF16 = jnp.bfloat16
VMEM = pl.BlockSpec(memory_space=pltpu.VMEM)
SMEM = pl.BlockSpec(memory_space=pltpu.SMEM)
PARAMS = pltpu.CompilerParams(vmem_limit_bytes=24 << 20)


def nn(left, right):
    return jnp.dot(left, right, preferred_element_type=F32)


def nt(left, right):
    return lax.dot_general(left, right, (((1,), (1,)), ((), ())), preferred_element_type=F32)


def tn(left, right):
    return lax.dot_general(left, right, (((0,), (0,)), ((), ())), preferred_element_type=F32)


def call(kernel, outs, args, scratch=(), smem=0):
    specs = [SMEM] * smem + [VMEM] * (len(args) - smem)
    out_shape = tuple(jax.ShapeDtypeStruct(s, d) for s, d in outs)
    return pl.pallas_call(
        kernel,
        in_specs=specs,
        out_specs=tuple(VMEM for _ in outs),
        out_shape=out_shape,
        scratch_shapes=[pltpu.VMEM(s, d) for s, d in scratch],
        compiler_params=PARAMS,
    )(*args)


def blocks(total, size):
    return [slice(i, i + size) for i in range(0, total, size)]


def entry_kernel(time_ref, source_ref, target_ref, feature_ref, out_ref):
    for batch in range(2):
        rows = slice(batch * 64, batch * 64 + 64)
        t = time_ref[batch]
        for q in range(SECTIONS):
            cols = slice(q * 1024, q * 1024 + 1024)
            source = source_ref[q, rows, :].astype(F32)
            target = target_ref[rows, cols].astype(F32)
            feature = feature_ref[batch : batch + 1, cols]
            out_ref[rows, cols] = ((1.0 - t) * source + t * target + feature).astype(BF16)


def forward_body(plane, x0, squeezed_in, widths, gain, frozen, into, onto, back, xs, normed):
    total = jnp.zeros((TOKENS, 1), F32)
    for cols in blocks(WIDTH, WIDE):
        x = x0[:, cols].astype(F32)
        for j in range(SECTIONS - 1):
            x = (x + nn(squeezed_in[j], widths[j, :, cols])).astype(BF16).astype(F32)
        xs[:, cols] = x.astype(BF16)
        total = total + jnp.sum(x * x, axis=1, keepdims=True)
    inverse = lax.rsqrt(total * (1.0 / WIDTH) + EPSILON)
    lowered = jnp.zeros((TOKENS, RANK), F32)
    for cols in blocks(WIDTH, WIDE):
        value = (xs[:, cols].astype(F32) * inverse * gain[:, cols]).astype(BF16)
        normed[:, cols] = value
        lowered = lowered + nt(value, into[:, cols])
    lowered = lowered.astype(BF16)
    return inverse, lowered


def forward_kernel(plane, x0, squeezed_in, widths, gain, frozen, into, onto, back, out, xs, normed):
    _, lowered = forward_body(plane, x0, squeezed_in, widths, gain, frozen, into, onto, back, xs, normed)
    squeezed = jnp.zeros((TOKENS, RANK), F32)
    for cols in blocks(HIDDEN, NARROW):
        pre = nn(normed[...], frozen[:, cols]) + nn(lowered, onto[:, cols])
        hidden = (pre * jax.nn.sigmoid(pre)).astype(BF16)
        squeezed = squeezed + nt(hidden, back[:, cols])
    squeezed = squeezed.astype(BF16)
    for j in range(SECTIONS - 1):
        out[j] = jnp.where(plane[0] == j, squeezed, squeezed_in[j])


def forward_last_kernel(
    plane, x0, squeezed_in, widths, gain, frozen, into, onto, back, own_width, source, target,
    xs, normed, inverse_out, lowered_out, slope, hidden_out, squeezed_out, seed, projected,
):
    inverse, lowered = forward_body(plane, x0, squeezed_in, widths, gain, frozen, into, onto, back, xs, normed)
    inverse_out[...] = inverse
    lowered_out[...] = lowered
    squeezed = jnp.zeros((TOKENS, RANK), F32)
    for cols in blocks(HIDDEN, NARROW):
        pre = nn(normed[...], frozen[:, cols]) + nn(lowered, onto[:, cols])
        sigmoid = jax.nn.sigmoid(pre)
        hidden = (pre * sigmoid).astype(BF16)
        slope[:, cols] = sigmoid * (1.0 + pre * (1.0 - sigmoid))
        hidden_out[:, cols] = hidden
        squeezed = squeezed + nt(hidden, back[:, cols])
    squeezed = squeezed.astype(BF16)
    squeezed_out[...] = squeezed
    scale = 8192.0 ** (-0.5)
    sums = [jnp.zeros((TOKENS, RANK), F32) for _ in range(SECTIONS)]
    for i, cols in enumerate(blocks(WIDTH, WIDE)):
        prediction = (xs[:, cols].astype(F32) + nn(squeezed, own_width[:, cols])).astype(BF16).astype(F32)
        part = slice((i % 2) * WIDE, (i % 2) * WIDE + WIDE)
        velocity = target[:, cols].astype(F32) - source[i // 2, :, part].astype(F32)
        value = ((prediction - velocity) * scale).astype(BF16)
        seed[:, cols] = value
        for j in range(SECTIONS):
            sums[j] = sums[j] + nt(value, widths[j, :, cols])
    for j in range(SECTIONS):
        projected[j] = sums[j]


def backward_body(plane, received, projected, back, slope, onto, frozen, into, xs, inverse, gain, d_pre, d_unit, gain_out):
    last = plane[0] == SECTIONS - 1
    own = received[jnp.minimum(plane[0], SECTIONS - 2)]
    d_squeezed = jnp.where(last, projected[SECTIONS - 1], own).astype(BF16)
    d_lowered = jnp.zeros((TOKENS, RANK), F32)
    for cols in blocks(HIDDEN, NARROW):
        value = (nn(d_squeezed, back[:, cols]) * slope[:, cols]).astype(BF16)
        d_pre[:, cols] = value
        d_lowered = d_lowered + nt(value, onto[:, cols])
    d_lowered = d_lowered.astype(BF16)
    total = jnp.zeros((TOKENS, 1), F32)
    for cols in blocks(WIDTH, WIDE):
        d_normed = nt(d_pre[...], frozen[cols, :]) + nn(d_lowered, into[:, cols])
        unit = xs[:, cols].astype(F32) * inverse[...]
        if gain_out is not None:
            gain_out[:, cols] = jnp.sum(d_normed * unit, axis=0, keepdims=True)
        else:
            value = d_normed * gain[:, cols]
            d_unit[:, cols] = value
            total = total + jnp.sum(value * unit, axis=1, keepdims=True)
    return d_squeezed, d_lowered, total


def backward_kernel(
    plane, received, projected, back, slope, onto, frozen, into, xs, inverse, gain, widths,
    out, d_stream, d_pre,
):
    _, _, total = backward_body(
        plane, received, projected, back, slope, onto, frozen, into, xs, inverse, gain, d_pre, d_stream, None
    )
    mean = total * (1.0 / WIDTH)
    sums = [jnp.zeros((TOKENS, RANK), F32) for _ in range(SECTIONS - 1)]
    for cols in blocks(WIDTH, WIDE):
        unit = xs[:, cols].astype(F32) * inverse[...]
        value = inverse[...] * (d_stream[:, cols] - unit * mean)
        d_stream[:, cols] = value
        narrow = value.astype(BF16)
        for j in range(SECTIONS - 1):
            sums[j] = sums[j] + nt(narrow, widths[j, :, cols])
    last = plane[0] == SECTIONS - 1
    for j in range(SECTIONS - 1):
        out[j] = jnp.where(last, projected[j], received[j]) + sums[j]


def backward_last_kernel(
    plane, received, projected, back, slope, onto, frozen, into, xs, inverse, gain, normed, lowered, hidden,
    keep, send, d_pre, gain_row, grads,
):
    d_squeezed, d_lowered, _ = backward_body(
        plane, received, projected, back, slope, onto, frozen, into, xs, inverse, gain, d_pre, None, gain_row
    )
    for cols in blocks(WIDTH, WIDE):
        grads[:, cols] = tn(d_lowered, normed[:, cols])
    for cols in blocks(HIDDEN, WIDE):
        grads[:, 4096 + cols.start : 4096 + cols.stop] = tn(lowered[...], d_pre[:, cols])
        grads[:, 6144 + cols.start : 6144 + cols.stop] = tn(d_squeezed, hidden[:, cols])
    grads[:, 8192:9216] = jnp.zeros((RANK, 1024), F32)
    for q in range(4):
        grads[q : q + 1, 8192:9216] = gain_row[:, q * 1024 : q * 1024 + 1024]
    half = grads.shape[1] // 2
    core = plane[1]
    keep[...] = grads[:, pl.ds(pl.multiple_of(core * half, 128), half)]
    send[...] = grads[:, pl.ds(pl.multiple_of((1 - core) * half, 128), half)]


def outward_kernel(plane, squeezed, cotangent, keep, send, grads):
    for cols in blocks(WIDTH, WIDE):
        grads[:, cols] = tn(squeezed[...], cotangent[:, cols])
    half = grads.shape[1] // 2
    core = plane[1]
    keep[...] = grads[:, pl.ds(pl.multiple_of(core * half, 128), half)]
    send[...] = grads[:, pl.ds(pl.multiple_of((1 - core) * half, 128), half)]


def exchange(x, axis):
    return lax.all_to_all(x, axis, split_axis=0, concat_axis=0, tiled=True)


def copies(x, count):
    return jnp.broadcast_to(x[None], (count,) + x.shape)


SWAP = [(0, 1), (1, 0)]


def summed_over_dp(keep, send):
    columns = keep.shape[1] // 4
    mine = keep + lax.ppermute(send, "core", SWAP)
    parts = mine.reshape(RANK, 4, columns).transpose(1, 0, 2)
    along_x = jnp.sum(exchange(parts, "x"), axis=0)
    along_z = jnp.sum(exchange(along_x.reshape(8, 8, columns), "z"), axis=0)
    rows = exchange(copies(along_z, 8), "z").reshape(RANK, columns)
    half = exchange(copies(rows, 4), "x").transpose(1, 0, 2).reshape(RANK, 4 * columns)
    other = lax.ppermute(half, "core", SWAP)
    first = lax.axis_index("core") == 0
    return jnp.concatenate([jnp.where(first, half, other), jnp.where(first, other, half)], axis=1)


def per_device(
    perturbed,
    control_token_states,
    owners,
    matched_control_row,
    cell_time_bins,
    frozen,
    section_norm_gain,
    adapter_into_rank,
    adapter_onto_hidden,
    adapter_hidden_to_rank,
    adapter_to_width,
):
    plane = lax.axis_index("pipe")
    position = lax.axis_index(DP)
    places = jnp.stack([plane, lax.axis_index("core")]).astype(jnp.int32)

    weights = lax.all_gather(frozen[0], DP, axis=0, tiled=True)

    names = owners[:, :, 0]
    same = (names[:, :, None] == names[:, None, :]) & jnp.tril(jnp.ones((64, 64), bool), -1)[None]
    rank = jnp.sum(same.astype(jnp.int32), axis=2)
    batch = jnp.arange(2, dtype=jnp.int32)[:, None]
    slot = (names * 8 + batch * 4 + rank).reshape(TOKENS)
    row = (batch * 64 + matched_control_row).reshape(TOKENS)
    chosen = slot[:, None] == jnp.arange(512, dtype=jnp.int32)[None, :]
    table = jnp.sum(jnp.where(chosen, row[:, None], 0), axis=0).reshape(64, 8)
    asked = exchange(table, DP).reshape(512)

    pool = control_token_states.reshape(TOKENS, WIDTH)
    quarter = lax.dynamic_slice_in_dim(pool, plane * 1024, 1024, axis=1)
    picked = nn((asked[:, None] == jnp.arange(TOKENS, dtype=jnp.int32)[None, :]).astype(BF16), quarter)
    arrived = exchange(picked.astype(BF16).reshape(64, 8, 1024), DP).reshape(512, 1024)
    own_quarter = nn(chosen.astype(BF16), arrived).astype(BF16)
    source = exchange(copies(own_quarter, SECTIONS), "pipe")
    widths = exchange(copies(adapter_to_width[0], SECTIONS), "pipe")

    cell = position // 32
    bins = jnp.where(cell == 0, cell_time_bins[:, 0], cell_time_bins[:, 1])
    t_val = (bins.astype(F32) + 0.5) / NBINS
    frequency = jnp.exp(-jnp.log(10000.0) * jnp.arange(WIDTH // 2, dtype=F32) / (WIDTH // 2))
    angles = (t_val * 1000.0)[:, None] * frequency[None, :]
    features = jnp.concatenate([jnp.sin(angles), jnp.cos(angles)], axis=1)
    target = perturbed.reshape(TOKENS, WIDTH)
    (x0,) = call(entry_kernel, [((TOKENS, WIDTH), BF16)], [t_val, source, target, features], smem=1)

    gain = section_norm_gain
    into = adapter_into_rank[0].T
    onto = adapter_onto_hidden[0]
    back = adapter_hidden_to_rank[0].T
    own_width = adapter_to_width[0]
    stream = ((TOKENS, WIDTH), BF16)
    down = [(i, i + 1) for i in range(SECTIONS - 1)]
    up = [(i + 1, i) for i in range(SECTIONS - 1)]

    squeezed_in = jnp.zeros((SECTIONS - 1, TOKENS, RANK), BF16)
    for _ in range(SECTIONS - 1):
        (squeezed_out,) = call(
            forward_kernel,
            [((SECTIONS - 1, TOKENS, RANK), BF16)],
            [places, x0, squeezed_in, widths, gain, weights, into, onto, back],
            scratch=[stream, stream],
            smem=1,
        )
        squeezed_in = lax.ppermute(squeezed_out, "pipe", down)
    xs, normed, inverse, lowered, slope, hidden, squeezed, seed, projected = call(
        forward_last_kernel,
        [
            stream,
            stream,
            ((TOKENS, 1), F32),
            ((TOKENS, RANK), BF16),
            ((TOKENS, HIDDEN), F32),
            ((TOKENS, HIDDEN), BF16),
            ((TOKENS, RANK), BF16),
            stream,
            ((SECTIONS, TOKENS, RANK), F32),
        ],
        [places, x0, squeezed_in, widths, gain, weights, into, onto, back, own_width, source, target],
        smem=1,
    )

    is_last = plane == SECTIONS - 1
    received = jnp.zeros((SECTIONS - 1, TOKENS, RANK), F32)
    cotangent = seed
    for _ in range(SECTIONS - 1):
        sent, d_stream = call(
            backward_kernel,
            [((SECTIONS - 1, TOKENS, RANK), F32), ((TOKENS, WIDTH), F32)],
            [places, received, projected, back, slope, onto, weights, into, xs, inverse, gain, widths],
            scratch=[((TOKENS, HIDDEN), BF16)],
            smem=1,
        )
        received = lax.ppermute(sent, "pipe", up)
        handed = (cotangent.astype(F32) + d_stream).astype(BF16)
        cotangent = jnp.where(is_last, seed, lax.ppermute(handed, "pipe", up))
    keep, send = call(
        backward_last_kernel,
        [((RANK, 4608), F32)] * 2,
        [places, received, projected, back, slope, onto, weights, into, xs, inverse, gain, normed, lowered, hidden],
        scratch=[((TOKENS, HIDDEN), BF16), ((1, WIDTH), F32), ((RANK, 9216), F32)],
        smem=1,
    )
    inner = summed_over_dp(keep, send)
    keep, send = call(
        outward_kernel,
        [((RANK, 2048), F32)] * 2,
        [places, squeezed, cotangent],
        scratch=[((RANK, WIDTH), F32)],
        smem=1,
    )
    outer = summed_over_dp(keep, send)
    return (
        inner[:4, 8192:].reshape(1, WIDTH),
        inner[:, :4096].T[None],
        inner[:, 4096:6144][None],
        inner[:, 6144:8192].T[None],
        outer[None],
    )


def solution(mesh):
    cells = Mesh(mesh.devices.reshape(8, 4, 2, 4), ("z", "x", "core", "pipe"))
    in_specs = (
        P(None, DP, None),
        P(None, DP, None),
        P(None, DP, None),
        P(None, DP),
        P(),
        P("pipe", DP, None),
        P("pipe", None),
        P("pipe", None, None),
        P("pipe", None, None),
        P("pipe", None, None),
        P("pipe", None, None),
    )
    out_specs = (
        P("pipe", None),
        P("pipe", None, None),
        P("pipe", None, None),
        P("pipe", None, None),
        P("pipe", None, None),
    )
    return jax.shard_map(per_device, mesh=cells, in_specs=in_specs, out_specs=out_specs, check_vma=False)
```

time: 676 us -> 464 us (0.69)
  blocking collectives: 249 us -> 75 us
  matrix products: 133 us -> 0.83 us
  Pallas kernels: 0 us -> 60.5 us
  starting transfers between devices: 59 us -> 84.8 us
  other arithmetic: 36.7 us -> 16.1 us
  local copies, waits for them, and re-layouts: 37 us -> 57.6 us
  waiting for transfers between devices: 133 us -> 146 us
    psum x1 -> x0, blocking collectives: 249 us -> none  [per_device(): lax.psum((gradient_totals[0], gradient_totals[1], gradient_totals[2], gra...]
    dot_general x70 -> x2, matrix products: 133 us -> 0.83 us  [nn(): return jnp.dot(left, right, preferred_element_type=F32)]
    all_to_all x0 -> x4, blocking collectives: none -> 75 us  [exchange(): return lax.all_to_all(x, axis, split_axis=0, concat_axis=0, tiled=True)]
    pallas_call x0 -> x10, Pallas kernels: none -> 60.5 us  [call(): pl.pallas_call(kernel, in_specs=specs, out_specs=tuple((VMEM for _ in out...]
    unnamed x89 -> x112, local copies, waits for them, and re-layouts: 10.6 us -> 49.1 us
    ppermute x8 -> x13, waiting for transfers between devices: 43.3 us -> 78 us  [the longest x3 50.3 us: per_device(): received = lax.ppermute(sent, 'pipe', up)]
    ppermute x8 -> x13, starting transfers between devices: 22.4 us -> 43.6 us  [the longest x2 16.1 us: summed_over_dp(): other = lax.ppermute(half, 'core', SWAP)]
    all_gather x1, waiting for transfers between devices: 20.5 us -> 0.01 us  [per_device(): weights = lax.all_gather(frozen[0], DP, axis=0, tiled=True)]
  transfers between devices with their start and end apart: 14 -> 22, of which waited for: 12 -> 16; matrix products, arithmetic and copies ran while one was open for 14% -> 3% of each run, Pallas kernels for 0% -> 6%
where the time goes in v1:
time: 464 us; the launch traced here: 455 us
  waiting for transfers between devices  146 us (31%)
  starting transfers between devices  84.8 us (18%)
  blocking collectives  75 us (16%)
  Pallas kernels  60.5 us (13%)
  local copies, waits for them, and re-layouts  57.6 us (12%)
  other arithmetic  16.1 us (3%)
  between operations  15.1 us (3%)
    all_to_all x4, blocking collectives, exchange(): return lax.all_to_all(x, axis, split_axis=0, concat_axis=0, tiled=True)  75 us
    all_to_all x8, waiting for transfers between devices, exchange(): return lax.all_to_all(x, axis, split_axis=0, concat_axis=0, tiled=True)  66.9 us
    pallas_call x10, Pallas kernels, call(): pl.pallas_call(kernel, in_specs=specs, out_specs=tuple((VMEM for _ in out...  60.5 us
    ppermute x3, waiting for transfers between devices, per_device(): received = lax.ppermute(sent, 'pipe', up)  50.3 us
    unnamed x112, local copies, waits for them, and re-layouts  49.1 us
    all_to_all x8, starting transfers between devices, exchange(): return lax.all_to_all(x, axis, split_axis=0, concat_axis=0, tiled=True)  41.2 us
    ppermute x3, waiting for transfers between devices, per_device(): cotangent = jnp.where(is_last, seed, lax.ppermute(handed, 'pipe', up))  20.5 us
    ppermute x2, starting transfers between devices, summed_over_dp(): other = lax.ppermute(half, 'core', SWAP)  16.1 us
  transfers between devices with their start and end apart: 22, of which 16 were waited for; matrix products, arithmetic and copies ran while one was open for 3% of the time, Pallas kernels for 6%

profile of v1, /device:TPU:1, one launch (start us, length us, event | category | flops | bytes accessed | tf_op | source)
XLA Modules:
  0.0 455.5 jit_solution(5646362942736353899)
XLA Ops:
  11.6 13.0 %all-to-all-start = ((s32[64,1,8]{2,1,0:T(1,128)}), s32[64,1,8]{2,1,0:T(1,128)S(1)}, u32[]{:S(2)}, u32[]{:S(2)}) async-start(s32[64,1,8]{2,1,0:T(1,128)} %bitcast.3), calls=%async_computation | async-start | bytes 65536 | tf_op jit(solution)/shard_map/all_to_all | solution.py:203
  24.6 9.3 %all-to-all-done = s32[64,1,8]{2,1,0:T(1,128)S(1)} async-done(((s32[64,1,8]{2,1,0:T(1,128)}), s32[64,1,8]{2,1,0:T(1,128)S(1)}, u32[]{:S(2)}, u32[]{:S(2)}) %all-to-all-start) | async-done | bytes 2080 | tf_op jit(solution)/shard_map/all_to_all | solution.py:203
  35.8 37.0 %all_to_all.64 = bf16[64,8,1024]{2,1,0:T(8,128)(2,1)S(1)} all-to-all(bf16[64,8,1024]{2,1,0:T(8,128)(2,1)S(1)} %fusion), channel_id=1, replica_groups=mesh['z'=8,'x'=4,'core'=2,'pipe'=4] {'z','x','core'}, dimensions={0} | all-to-all | bytes 2097152 | tf_op jit(solution)/shard_map/all_to_all | solution.py:203
  73.3 18.3 %all_to_all.65.source_ref.source = bf16[4,128,1024]{2,1,0:T(8,128)(2,1)} all-to-all(bf16[4,128,1024]{2,1,0:T(8,128)(2,1)S(1)} %broadcast_in_dim.84), channel_id=1, replica_groups=mesh['z'=8,'x'=4,'core'=2,'pipe'=4] {'pipe'}, dimensions={0} | all-to-all | bytes 2097152 | tf_op jit(solution)/shard_map/all_to_all | solution.py:203
  102.2 19.2 %all-to-all-done.3.widths = bf16[4,64,4096]{2,1,0:T(8,128)(2,1)S(1)} async-done(((bf16[4,64,4096]{2,1,0:T(8,128)(2,1)}), bf16[4,64,4096]{2,1,0:T(8,128)(2,1)S(1)}, u32[]{:S(2)}, u32[]{:S(2)}) %all-to-all-start.3) | async-done | bytes 2097184 | tf_op jit(solution)/shard_map/all_to_all | solution.py:203
  121.4 6.5 %copy-done.2 = bf16[1,4096,2048]{2,1,0:T(8,128)(2,1)S(1)} copy-done((bf16[1,4096,2048]{2,1,0:T(8,128)(2,1)S(1)}, bf16[1,4096,2048]{2,1,0:T(8,128)(2,1)}, u32[]{:S(2)}) %copy-start.2) | copy-done | bytes 16777240
  129.1 5.8 %shard_map.147 = bf16[3,128,64]{2,1,0:T(8,128)(2,1)S(1)} custom-call(s32[2]{0:T(128)S(1)} %pad_add_fusion.plane, bf16[128,4096]{1,0:T(8,128)(2,1)S(1)} %copy-done.13, bf16[3,128,64]{2,1,0:T(8,128)(2,1)S(1)} %broadcast_in_dim.85.squeezed_in, bf16[4,64,4096]{2,1,0:T(8,128)(2,1)S(1)} %all-to-all-done.3.widths, f32[1,4096]{1,0:T(1,128)S(1)} %copy-done.43, ...), custom_call_target="tpu_custom_call" | custom-call | tf_op jit(solution)/shard_map/pallas_call | solution.py:41
  138.7 5.8 %shard_map.148 = bf16[3,128,64]{2,1,0:T(8,128)(2,1)S(1)} custom-call(s32[2]{0:T(128)S(1)} %pad_add_fusion.plane, bf16[128,4096]{1,0:T(8,128)(2,1)S(1)} %copy-done.13, bf16[3,128,64]{2,1,0:T(8,128)(2,1)S(1)} %collective-permute-done.squeezed_in, bf16[4,64,4096]{2,1,0:T(8,128)(2,1)S(1)} %all-to-all-done.3.widths, f32[1,4096]{1,0:T(1,128)S(1)} %copy-done.43, ...), custom_call_target="tpu_custom_call" | custom-call | tf_op jit(solution)/shard_map/pallas_call | solution.py:41
  150.1 5.8 %shard_map.149 = bf16[3,128,64]{2,1,0:T(8,128)(2,1)S(1)} custom-call(s32[2]{0:T(128)S(1)} %pad_add_fusion.plane, bf16[128,4096]{1,0:T(8,128)(2,1)S(1)} %copy-done.13, bf16[3,128,64]{2,1,0:T(8,128)(2,1)S(1)} %collective-permute-done.1.squeezed_in, bf16[4,64,4096]{2,1,0:T(8,128)(2,1)S(1)} %all-to-all-done.3.widths, f32[1,4096]{1,0:T(1,128)S(1)} %copy-done.43, ...), custom_call_target="tpu_custom_call" | custom-call | tf_op jit(solution)/shard_map/pallas_call | solution.py:41
  161.2 5.8 %copy-done.4 = bf16[1,4096,2048]{2,1,0:T(8,128)(2,1)S(1)} copy-done((bf16[1,4096,2048]{2,1,0:T(8,128)(2,1)S(1)}, bf16[1,4096,2048]{2,1,0:T(8,128)(2,1)}, u32[]{:S(2)}) %copy-start.4) | copy-done | bytes 16777240
  168.2 8.0 %shard_map.150 = (bf16[128,4096]{1,0:T(8,128)(2,1)S(1)}, bf16[128,4096]{1,0:T(8,128)(2,1)S(1)}, f32[128,1]{1,0:T(8,128)S(1)}, bf16[128,64]{1,0:T(8,128)(2,1)S(1)...) custom-call(s32[2]{0:T(128)S(1)} %pad_add_fusion.plane, ...), custom_call_target="tpu_custom_call" | custom-call | tf_op jit(solution)/shard_map/pallas_call | solution.py:41
  178.7 7.0 %copy-done.5 = bf16[1,4096,2048]{2,1,0:T(8,128)(2,1)S(1)} copy-done((bf16[1,4096,2048]{2,1,0:T(8,128)(2,1)S(1)}, bf16[1,4096,2048]{2,1,0:T(8,128)(2,1)}, u32[]{:S(2)}) %copy-start.5) | copy-done | bytes 16777240
  185.7 8.9 %shard_map.151 = (f32[3,128,64]{2,1,0:T(8,128)}, f32[128,4096]{1,0:T(8,128)S(1)}) custom-call(s32[2]{0:T(128)S(1)} %pad_add_fusion.plane, f32[3,128,64]{2,1,0:T(8,128)S(1)} %broadcast_in_dim.80.received, f32[4,128,64]{2,1,0:T(8,128)S(1)} %get-tuple-element.24.projected, bf16[64,2048]{1,0:T(8,128)(2,1)S(1)} %bitcast.91, ...), custom_call_target="tpu_custom_call" | custom-call | tf_op jit(solution)/shard_map/pallas_call | solution.py:41
  198.6 22.6 %collective-permute-done.3.received = f32[3,128,64]{2,1,0:T(8,128)} collective-permute-done((f32[3,128,64]{2,1,0:T(8,128)}, f32[3,128,64]{2,1,0:T(8,128)}, u32[]{:S(2)}, u32[]{:S(2)}) %collective-permute-start.3) | collective-permute-done | bytes 98336 | tf_op jit(solution)/shard_map/ppermute | solution.py:319
  221.2 5.8 %copy-done.6 = bf16[1,4096,2048]{2,1,0:T(8,128)(2,1)S(1)} copy-done((bf16[1,4096,2048]{2,1,0:T(8,128)(2,1)S(1)}, bf16[1,4096,2048]{2,1,0:T(8,128)(2,1)}, u32[]{:S(2)}) %copy-start.6) | copy-done | bytes 16777240
  229.4 8.7 %shard_map.152 = (f32[3,128,64]{2,1,0:T(8,128)S(1)}, f32[128,4096]{1,0:T(8,128)S(1)}) custom-call(s32[2]{0:T(128)S(1)} %pad_add_fusion.plane, f32[3,128,64]{2,1,0:T(8,128)} %collective-permute-done.3.received, f32[4,128,64]{2,1,0:T(8,128)S(1)} %get-tuple-element.24.projected, bf16[64,2048]{1,0:T(8,128)(2,1)S(1)} %bitcast.92, f32[128,2048]{1,0:T(8,128)S(1)} %copy-done.25, ...), custom_call_target="tpu_custom_call" | custom-call | tf_op jit(solution)/shard_map/pallas_call | solution.py:41
  243.8 21.2 %collective-permute-done.4.received = f32[3,128,64]{2,1,0:T(8,128)S(1)} collective-permute-done((f32[3,128,64]{2,1,0:T(8,128)S(1)}, f32[3,128,64]{2,1,0:T(8,128)S(1)}, u32[]{:S(2)}, u32[]{:S(2)}) %collective-permute-start.4) | collective-permute-done | bytes 98336 | tf_op jit(solution)/shard_map/ppermute | solution.py:319
  267.6 8.2 %shard_map.153 = (f32[3,128,64]{2,1,0:T(8,128)S(1)}, f32[128,4096]{1,0:T(8,128)S(1)}) custom-call(s32[2]{0:T(128)S(1)} %pad_add_fusion.plane, f32[3,128,64]{2,1,0:T(8,128)S(1)} %copy-done.47, f32[4,128,64]{2,1,0:T(8,128)S(1)} %copy-done.33, bf16[64,2048]{1,0:T(8,128)(2,1)S(1)} %bitcast.93, f32[128,2048]{1,0:T(8,128)S(1)} %copy-done.25, ...), custom_call_target="tpu_custom_call" | custom-call | tf_op jit(solution)/shard_map/pallas_call | solution.py:41
  278.7 6.5 %collective-permute-done.5.received = f32[3,128,64]{2,1,0:T(8,128)S(1)} collective-permute-done((f32[3,128,64]{2,1,0:T(8,128)S(1)}, f32[3,128,64]{2,1,0:T(8,128)S(1)}, u32[]{:S(2)}, u32[]{:S(2)}) %collective-permute-start.5) | collective-permute-done | bytes 98336 | tf_op jit(solution)/shard_map/ppermute | solution.py:319
  293.8 7.4 %shard_map.154 = (f32[64,4608]{1,0:T(8,128)S(1)}, f32[64,4608]{1,0:T(8,128)S(1)}) custom-call(s32[2]{0:T(128)S(1)} %pad_add_fusion.plane, f32[3,128,64]{2,1,0:T(8,128)S(1)} %collective-permute-done.5.received, f32[4,128,64]{2,1,0:T(8,128)S(1)} %copy-done.34, bf16[64,2048]{1,0:T(8,128)(2,1)S(1)} %bitcast.94, f32[128,2048]{1,0:T(8,128)S(1)} %copy-done.26, ...), custom_call_target="tpu_custom_call" | custom-call | tf_op jit(solution)/shard_map/pallas_call | solution.py:41
  301.2 7.9 %collective-permute-start.6 = (f32[64,4608]{1,0:T(8,128)S(1)}, f32[64,4608]{1,0:T(8,128)S(1)}, u32[]{:S(2)}, u32[]{:S(2)}) collective-permute-start(f32[64,4608]{1,0:T(8,128)S(1)} %get-tuple-element.35), channel_id=1, source_target_pairs={{0,4},{4,0},{1,5},{5,1},{2,6},{6,2},{3,7},{7,3},{8,12},{12,8},{9,1... | collective-permute-start | bytes 3538952 | tf_op jit(solution)/shard_map/ppermute | solution.py:215
  314.4 4.2 all-to-all-start.4
  318.6 20.5 %collective-permute-done.10 = bf16[128,4096]{1,0:T(8,128)(2,1)S(1)} collective-permute-done((bf16[128,4096]{1,0:T(8,128)(2,1)}, bf16[128,4096]{1,0:T(8,128)(2,1)S(1)}, u32[]{:S(2)}, u32[]{:S(2)}) %collective-permute-start.10) | collective-permute-done | bytes 1048608 | tf_op jit(solution)/shard_map/ppermute | solution.py:321
  348.2 8.1 %all-to-all-done.8 = f32[4,64,512]{2,1,0:T(8,128)S(1)} async-done(((f32[4,64,512]{2,1,0:T(8,128)}), f32[4,64,512]{2,1,0:T(8,128)S(1)}, u32[]{:S(2)}, u32[]{:S(2)}) %all-to-all-start.8) | async-done | bytes 524320 | tf_op jit(solution)/shard_map/all_to_all | solution.py:203
  356.3 5.8 %all-to-all-start.5 = ((f32[8,8,1152]{2,1,0:T(8,128)}), f32[8,8,1152]{2,1,0:T(8,128)S(1)}, u32[]{:S(2)}, u32[]{:S(2)}) async-start(f32[8,8,1152]{2,1,0:T(8,128)} %bitcast.16), calls=%async_computation.5 | async-start | bytes 589824 | tf_op jit(solution)/shard_map/all_to_all | solution.py:203
  362.8 9.9 %all-to-all-done.5 = f32[8,8,1152]{2,1,0:T(8,128)S(1)} async-done(((f32[8,8,1152]{2,1,0:T(8,128)}), f32[8,8,1152]{2,1,0:T(8,128)S(1)}, u32[]{:S(2)}, u32[]{:S(2)}) %all-to-all-start.5) | async-done | bytes 294944 | tf_op jit(solution)/shard_map/all_to_all | solution.py:203
  376.2 7.8 %all-to-all-done.9 = f32[8,8,512]{2,1,0:T(8,128)S(1)} async-done(((f32[8,8,512]{2,1,0:T(8,128)}), f32[8,8,512]{2,1,0:T(8,128)S(1)}, u32[]{:S(2)}, u32[]{:S(2)}) %all-to-all-start.9) | async-done | bytes 131104 | tf_op jit(solution)/shard_map/all_to_all | solution.py:203
  388.2 9.7 %all-to-all-done.6 = f32[8,8,1152]{2,1,0:T(8,128)S(1)} async-done(((f32[8,8,1152]{2,1,0:T(8,128)}), f32[8,8,1152]{2,1,0:T(8,128)S(1)}, u32[]{:S(2)}, u32[]{:S(2)}) %all-to-all-start.6) | async-done | bytes 294944 | tf_op jit(solution)/shard_map/all_to_all | solution.py:203
  397.9 10.3 %all_to_all.66 = f32[8,8,512]{2,1,0:T(8,128)S(1)} all-to-all(f32[8,8,512]{2,1,0:T(8,128)S(1)} %broadcast_in_dim.94), channel_id=1, replica_groups=mesh['z'=8,'x'=4,'core'=2,'pipe'=4] {'z'}, dimensions={0} | all-to-all | bytes 262144 | tf_op jit(solution)/shard_map/all_to_all | solution.py:203
  408.2 9.3 %all_to_all.67 = f32[4,64,512]{2,1,0:T(8,128)S(1)} all-to-all(f32[4,64,512]{2,1,0:T(8,128)S(1)} %broadcast_in_dim.96), channel_id=1, replica_groups=mesh['z'=8,'x'=4,'core'=2,'pipe'=4] {'x'}, dimensions={0} | all-to-all | bytes 1048576 | tf_op jit(solution)/shard_map/all_to_all | solution.py:203
  422.3 7.5 %collective-permute-start.12 = (f32[64,2048]{1,0:T(8,128)S(1)}, f32[64,2048]{1,0:T(8,128)S(1)}, u32[]{:S(2)}, u32[]{:S(2)}) collective-permute-start(f32[64,2048]{1,0:T(8,128)S(1)} %bitcast.103), channel_id=1, source_target_pairs={{0,4},{4,0},{1,5},{5,1},{2,6},{6,2},{3,7},{7,3},{8,12},{12,8},{9,1... | collective-permute-start | bytes 1572872 | tf_op jit(solution)/shard_map/ppermute | solution.py:221
  432.7 8.6 %collective-permute-start.7 = (f32[64,4608]{1,0:T(8,128)S(1)}, f32[64,4608]{1,0:T(8,128)}, u32[]{:S(2)}, u32[]{:S(2)}) collective-permute-start(f32[64,4608]{1,0:T(8,128)S(1)} %bitcast.99), channel_id=1, source_target_pairs={{0,4},{4,0},{1,5},{5,1},{2,6},{6,2},{3,7},{7,3},{8,12},{12,8},{9,1... | collective-permute-start | bytes 3538952 | tf_op jit(solution)/shard_map/ppermute | solution.py:221
  (192 shorter events, 99.9 us)
Async XLA Ops:
  7.2 28.1 %copy-start = (bf16[2,64,4096]{2,1,0:T(8,128)(2,1)S(1)}, bf16[2,64,4096]{2,1,0:T(8,128)(2,1)}, u32[]{:S(2)}) copy-start(bf16[2,64,4096]{2,1,0:T(8,128)(2,1)} %param.12) | copy-start | bytes 3145732
  7.2 114.2 %all-gather.3.cloned.1.call-start = ((), (), s32[]{:S(2)}) async-start(), calls=%async_computation.12 | async-start | bytes 17039360 | tf_op jit(solution)/shard_map/all_gather | solution.py:243
  11.6 22.3 %all-to-all-start = ((s32[64,1,8]{2,1,0:T(1,128)}), s32[64,1,8]{2,1,0:T(1,128)S(1)}, u32[]{:S(2)}, u32[]{:S(2)}) async-start(s32[64,1,8]{2,1,0:T(1,128)} %bitcast.3), calls=%async_computation | async-start | bytes 65536 | tf_op jit(solution)/shard_map/all_to_all | solution.py:203
  93.2 28.2 %all-to-all-start.3 = ((bf16[4,64,4096]{2,1,0:T(8,128)(2,1)}), bf16[4,64,4096]{2,1,0:T(8,128)(2,1)S(1)}, u32[]{:S(2)}, u32[]{:S(2)}) async-start(bf16[4,64,4096]{2,1,0:T(8,128)(2,1)} %broadcast_in_dim.87), calls=%async_computation.3 | async-start | bytes 4194304 | tf_op jit(solution)/shard_map/all_to_all | solution.py:203
  121.4 99.8 %copy-start.7 = (bf16[4,64,4096]{2,1,0:T(8,128)(2,1)}, bf16[4,64,4096]{2,1,0:T(8,128)(2,1)S(1)}, u32[]{:S(2)}) copy-start(bf16[4,64,4096]{2,1,0:T(8,128)(2,1)S(1)} %all-to-all-done.3.widths) | copy-start | bytes 6291460
  135.0 3.8 collective-permute-start
  144.6 5.5 %collective-permute-start.1 = (bf16[3,128,64]{2,1,0:T(8,128)(2,1)S(1)}, bf16[3,128,64]{2,1,0:T(8,128)(2,1)S(1)}, u32[]{:S(2)}, u32[]{:S(2)}) collective-permute-start(bf16[3,128,64]{2,1,0:T(8,128)(2,1)S(1)} %shard_map.148), channel_id=1, source_target_pairs={{0,1},{1,2},{2,3},{4,5},{5,6},{6,7},{8,9},{9,10},{10,11},{12,13},{... | collective-permute-start | bytes 147464 | tf_op jit(solution)/shard_map/ppermute | solution.py:290
  155.9 5.4 %collective-permute-start.2 = (bf16[3,128,64]{2,1,0:T(8,128)(2,1)S(1)}, bf16[3,128,64]{2,1,0:T(8,128)(2,1)S(1)}, u32[]{:S(2)}, u32[]{:S(2)}) collective-permute-start(bf16[3,128,64]{2,1,0:T(8,128)(2,1)S(1)} %shard_map.149), channel_id=1, source_target_pairs={{0,1},{1,2},{2,3},{4,5},{5,6},{6,7},{8,9},{9,10},{10,11},{12,13},{... | collective-permute-start | bytes 147464 | tf_op jit(solution)/shard_map/ppermute | solution.py:290
  178.6 42.5 %copy-start.32 = (f32[4,128,64]{2,1,0:T(8,128)}, f32[4,128,64]{2,1,0:T(8,128)S(1)}, u32[]{:S(2)}) copy-start(f32[4,128,64]{2,1,0:T(8,128)S(1)} %get-tuple-element.24.projected) | copy-start | bytes 393220
  195.8 42.4 %collective-permute-start.8 = (bf16[128,4096]{1,0:T(8,128)(2,1)}, bf16[128,4096]{1,0:T(8,128)(2,1)}, u32[]{:S(2)}, u32[]{:S(2)}) collective-permute-start(bf16[128,4096]{1,0:T(8,128)(2,1)} %add_convert_fusion.2), channel_id=1, source_target_pairs={{1,0},{2,1},{3,2},{5,4},{6,5},{7,6},{9,8},{10,9},{11,10},{13,12},{... | collective-permute-start | bytes 3145736 | tf_op jit(solution)/shard_map/ppermute | solution.py:321
  197.1 24.1 %collective-permute-start.3 = (f32[3,128,64]{2,1,0:T(8,128)}, f32[3,128,64]{2,1,0:T(8,128)}, u32[]{:S(2)}, u32[]{:S(2)}) collective-permute-start(f32[3,128,64]{2,1,0:T(8,128)} %get-tuple-element.28), channel_id=1, source_target_pairs={{1,0},{2,1},{3,2},{5,4},{6,5},{7,6},{9,8},{10,9},{11,10},{13,12},{... | collective-permute-start | bytes 294920 | tf_op jit(solution)/shard_map/ppermute | solution.py:319
  229.4 36.4 %copy-start.10 = (bf16[1,4096,64]{1,2,0:T(8,128)(2,1)S(1)}, bf16[1,4096,64]{1,2,0:T(8,128)(2,1)}, u32[]{:S(2)}) copy-start(bf16[1,4096,64]{1,2,0:T(8,128)(2,1)} %param.18) | copy-start | bytes 1572868
  229.4 36.4 %copy-start.16 = (bf16[1,64,2048]{2,1,0:T(8,128)(2,1)S(1)}, bf16[1,64,2048]{2,1,0:T(8,128)(2,1)}, u32[]{:S(2)}) copy-start(bf16[1,64,2048]{2,1,0:T(8,128)(2,1)} %param.19) | copy-start | bytes 786436
  229.4 36.4 %copy-start.19 = (bf16[1,2048,64]{1,2,0:T(8,128)(2,1)S(1)}, bf16[1,2048,64]{1,2,0:T(8,128)(2,1)}, u32[]{:S(2)}) copy-start(bf16[1,2048,64]{1,2,0:T(8,128)(2,1)} %param.20) | copy-start | bytes 786436
  229.4 55.8 %slice-start = ((s8[16777216]{0:T(1024)(128)(4,1)}), s8[4194304]{0:T(1024)(128)(4,1)S(1)}, s32[]{:S(2)}) async-start(s8[16777216]{0:T(1024)(128)(4,1)} %bitcast.68), calls=%async_computation.13 | async-start | bytes 8388608
  229.4 55.8 %slice-start.1 = ((s8[16777216]{0:T(1024)(128)(4,1)}), s8[4194304]{0:T(1024)(128)(4,1)S(1)}, s32[]{:S(2)}) async-start(s8[16777216]{0:T(1024)(128)(4,1)} %bitcast.68), calls=%async_computation.14 | async-start | bytes 8388608
  238.2 47.1 %slice-start.2 = ((s8[16777216]{0:T(1024)(128)(4,1)}), s8[4194304]{0:T(1024)(128)(4,1)S(1)}, s32[]{:S(2)}) async-start(s8[16777216]{0:T(1024)(128)(4,1)} %bitcast.68), calls=%async_computation.15 | async-start | bytes 8388608
  241.0 68.2 %collective-permute-start.9 = (bf16[128,4096]{1,0:T(8,128)(2,1)}, bf16[128,4096]{1,0:T(8,128)(2,1)}, u32[]{:S(2)}, u32[]{:S(2)}) collective-permute-start(bf16[128,4096]{1,0:T(8,128)(2,1)} %add_convert_fusion.1), channel_id=1, source_target_pairs={{1,0},{2,1},{3,2},{5,4},{6,5},{7,6},{9,8},{10,9},{11,10},{13,12},{... | collective-permute-start | bytes 3145736 | tf_op jit(solution)/shard_map/ppermute | solution.py:321
  242.3 43.0 %slice-start.3 = ((s8[16777216]{0:T(1024)(128)(4,1)}), s8[4194304]{0:T(1024)(128)(4,1)S(1)}, s32[]{:S(2)}) async-start(s8[16777216]{0:T(1024)(128)(4,1)} %bitcast.68), calls=%async_computation.16 | async-start | bytes 8388608
  242.3 22.8 %collective-permute-start.4 = (f32[3,128,64]{2,1,0:T(8,128)S(1)}, f32[3,128,64]{2,1,0:T(8,128)S(1)}, u32[]{:S(2)}, u32[]{:S(2)}) collective-permute-start(f32[3,128,64]{2,1,0:T(8,128)S(1)} %get-tuple-element.29), channel_id=1, source_target_pairs={{1,0},{2,1},{3,2},{5,4},{6,5},{7,6},{9,8},{10,9},{11,10},{13,12},{... | collective-permute-start | bytes 294920 | tf_op jit(solution)/shard_map/ppermute | solution.py:319
  277.2 8.0 %collective-permute-start.5 = (f32[3,128,64]{2,1,0:T(8,128)S(1)}, f32[3,128,64]{2,1,0:T(8,128)S(1)}, u32[]{:S(2)}, u32[]{:S(2)}) collective-permute-start(f32[3,128,64]{2,1,0:T(8,128)S(1)} %get-tuple-element.30), channel_id=1, source_target_pairs={{1,0},{2,1},{3,2},{5,4},{6,5},{7,6},{9,8},{10,9},{11,10},{13,12},{... | collective-permute-start | bytes 294920 | tf_op jit(solution)/shard_map/ppermute | solution.py:319
  301.2 11.8 %collective-permute-start.6 = (f32[64,4608]{1,0:T(8,128)S(1)}, f32[64,4608]{1,0:T(8,128)S(1)}, u32[]{:S(2)}, u32[]{:S(2)}) collective-permute-start(f32[64,4608]{1,0:T(8,128)S(1)} %get-tuple-element.35), channel_id=1, source_target_pairs={{0,4},{4,0},{1,5},{5,1},{2,6},{6,2},{3,7},{7,3},{8,12},{12,8},{9,1... | collective-permute-start | bytes 3538952 | tf_op jit(solution)/shard_map/ppermute | solution.py:215
  311.8 27.3 %collective-permute-start.10 = (bf16[128,4096]{1,0:T(8,128)(2,1)}, bf16[128,4096]{1,0:T(8,128)(2,1)S(1)}, u32[]{:S(2)}, u32[]{:S(2)}) collective-permute-start(bf16[128,4096]{1,0:T(8,128)(2,1)} %add_convert_fusion), channel_id=1, source_target_pairs={{1,0},{2,1},{3,2},{5,4},{6,5},{7,6},{9,8},{10,9},{11,10},{13,12},{... | collective-permute-start | bytes 3145736 | tf_op jit(solution)/shard_map/ppermute | solution.py:321
  314.4 28.9 %all-to-all-start.4 = ((f32[4,64,1152]{2,1,0:T(8,128)}), f32[4,64,1152]{2,1,0:T(8,128)S(1)}, u32[]{:S(2)}, u32[]{:S(2)}) async-start(f32[4,64,1152]{2,1,0:T(8,128)} %bitcast.57), calls=%async_computation.4 | async-start | bytes 2359296 | tf_op jit(solution)/shard_map/all_to_all | solution.py:203
  340.2 2.2 collective-permute-start.11
  343.3 13.0 %all-to-all-start.8 = ((f32[4,64,512]{2,1,0:T(8,128)}), f32[4,64,512]{2,1,0:T(8,128)S(1)}, u32[]{:S(2)}, u32[]{:S(2)}) async-start(f32[4,64,512]{2,1,0:T(8,128)} %bitcast.59), calls=%async_computation.8 | async-start | bytes 1048576 | tf_op jit(solution)/shard_map/all_to_all | solution.py:203
  356.3 16.5 %all-to-all-start.5 = ((f32[8,8,1152]{2,1,0:T(8,128)}), f32[8,8,1152]{2,1,0:T(8,128)S(1)}, u32[]{:S(2)}, u32[]{:S(2)}) async-start(f32[8,8,1152]{2,1,0:T(8,128)} %bitcast.16), calls=%async_computation.5 | async-start | bytes 589824 | tf_op jit(solution)/shard_map/all_to_all | solution.py:203
  372.8 11.2 %all-to-all-start.9 = ((f32[8,8,512]{2,1,0:T(8,128)}), f32[8,8,512]{2,1,0:T(8,128)S(1)}, u32[]{:S(2)}, u32[]{:S(2)}) async-start(f32[8,8,512]{2,1,0:T(8,128)} %bitcast.25), calls=%async_computation.9 | async-start | bytes 262144 | tf_op jit(solution)/shard_map/all_to_all | solution.py:203
  384.7 13.1 %all-to-all-start.6 = ((f32[8,8,1152]{2,1,0:T(8,128)}), f32[8,8,1152]{2,1,0:T(8,128)S(1)}, u32[]{:S(2)}, u32[]{:S(2)}) async-start(f32[8,8,1152]{2,1,0:T(8,128)} %broadcast_in_dim.88), calls=%async_computation.6 | async-start | bytes 589824 | tf_op jit(solution)/shard_map/all_to_all | solution.py:203
  418.7 13.9 %all-to-all-start.7 = ((f32[4,64,1152]{2,1,0:T(8,128)}), f32[4,64,1152]{2,1,0:T(8,128)S(1)}, u32[]{:S(2)}, u32[]{:S(2)}) async-start(f32[4,64,1152]{2,1,0:T(8,128)} %broadcast_in_dim.90), calls=%async_computation.7 | async-start | bytes 2359296 | tf_op jit(solution)/shard_map/all_to_all | solution.py:203
  422.3 19.1 %collective-permute-start.12 = (f32[64,2048]{1,0:T(8,128)S(1)}, f32[64,2048]{1,0:T(8,128)S(1)}, u32[]{:S(2)}, u32[]{:S(2)}) collective-permute-start(f32[64,2048]{1,0:T(8,128)S(1)} %bitcast.103), channel_id=1, source_target_pairs={{0,4},{4,0},{1,5},{5,1},{2,6},{6,2},{3,7},{7,3},{8,12},{12,8},{9,1... | collective-permute-start | bytes 1572872 | tf_op jit(solution)/shard_map/ppermute | solution.py:221
  432.7 11.2 %collective-permute-start.7 = (f32[64,4608]{1,0:T(8,128)S(1)}, f32[64,4608]{1,0:T(8,128)}, u32[]{:S(2)}, u32[]{:S(2)}) collective-permute-start(f32[64,4608]{1,0:T(8,128)S(1)} %bitcast.99), channel_id=1, source_target_pairs={{0,4},{4,0},{1,5},{5,1},{2,6},{6,2},{3,7},{7,3},{8,12},{12,8},{9,1... | collective-permute-start | bytes 3538952 | tf_op jit(solution)/shard_map/ppermute | solution.py:221
  (45 other events, 369.2 us)
Sparse Core Ops, SparseCore 0:
  10.8 110.2 all-gather.2
